TPU v7x, 32 devices: a whole 2x2x4 slice. The times are simulated.
32 devices in a mesh: slab: 4 (over z), grp: 8 (over y, x, core).
Axes of the slice: x: 2, y: 2, z: 4, core: 2. Of those that a mesh axis runs over, the one named last changes fastest.
Arguments:
- samples: float32 [32768, 6, 128], P(('slab', 'grp')), as said below
- block_ids: int32 [32768], P(('slab', 'grp')), may hold values from 0 to 32767, as said below
- tile_counts: int32 [32768], P(('slab', 'grp')), may hold values from 0 to 128
- occupied: int32 [8, 16, 256], P('slab', 'grp'), may hold values 0 or 1
- coupling: float32 [27, 64, 64], replicated, may hold values from -0.06 to 0.06
Outputs:
- solution_field: float32 [64, 8, 16, 256], P(None, 'slab', 'grp')
- residual: float32 [64, 8, 16, 256], P(None, 'slab', 'grp')
Inputs may be any that keep to these rules, and one draw needn't show every extreme that they name: `samples`: the first three components of every sample lie in [0, 1). `block_ids`: slot j * 32 + c of a device's slots (c below 32) carries a block whose x // 2 is the slab index and y // 2 the grp index of the device of linear index j over slab then grp; ids number blocks as (x * 16 + y) * 256 + z; every block is named by exactly one slot over all devices.
All inputs are finite; a program needn't handle non-finite values. No bound on the sum of `occupied` on one device may be relied on, other than what follows from the above.
Results may differ from a plain program's by a relative error of at most 0.0003.
Values sent between devices are 32-bit elements; how exact they have to be, the bound alone decides.
A program may use at most 128 MiB of HBM per device.

v0:
```python
import functools

import jax
import jax.numpy as jnp
from jax import lax
from jax.experimental import pallas as pl
from jax.experimental.pallas import tpu as pltpu
from jax.sharding import PartitionSpec as P

ITERS = 3
MESH = pl.DeviceIdType.MESH
F32 = jnp.float32
BF16 = jnp.bfloat16


def hats(u):
    hat, low = [], []
    for j in range(5):
        g = u - float(j)
        h = jnp.maximum(1.0 - jnp.abs(g), 0.0)
        hat.append(h)
        low.append((0.5 + 0.5 * g) * h)
    values = [low[i] + (hat[i + 1] - low[i + 1]) for i in range(4)]
    slopes = [hat[i] - hat[i + 1] for i in range(4)]
    return values, slopes


def split(x):
    hi = x.astype(BF16)
    return hi, (x - hi.astype(F32)).astype(BF16)


def total(x):
    return jnp.sum(jnp.sum(x, axis=0, keepdims=True), axis=1, keepdims=True)


def kernel(n_slab, n_grp, samples, counts, idrows, occupied, coupling, x_out, r_out,
           fac, nodes, send, recv, cs, chi, clo, diag, halo_out, halo_in, image, res, wvec,
           zvec, dvec, qvec, zq, part, parts, weights, a2a_send, a2a_recv, halo_send, halo_recv,
           sum_send, sum_recv):
    devs = n_slab * n_grp
    cap = send.shape[1] - 8
    per = 128 // cap
    groups = samples.shape[0] // 128
    slab = lax.axis_index("slab")
    grp = lax.axis_index("grp")
    me = slab * n_grp + grp

    part[...] = jnp.zeros_like(part)
    barrier = pltpu.get_barrier_semaphore()

    def greet(k, carry):
        other = lax.rem(me + k, devs)
        pl.semaphore_signal(barrier, inc=1, device_id=(other // n_grp, lax.rem(other, n_grp)),
                            device_id_type=MESH)
        return carry

    lax.fori_loop(1, devs, greet, 0)
    pl.semaphore_wait(barrier, devs - 1)

    def splat(step, carry):
        g = lax.rem(me // per + groups // 2 + step, groups)
        rows = pl.ds(pl.multiple_of(g * 128, 128), 128)
        live = lax.broadcasted_iota(jnp.int32, (128, 128), 0) < counts[g]
        for d in range(3):
            values, slopes = hats(4.0 * samples[rows, d, :].T)
            normal = 4.0 * samples[rows, 3 + d, :].T
            if d == 0:
                normal = jnp.where(live, normal, 0.0)
            for i in range(4):
                fac[8 * d + i] = jnp.where(live, values[i], 0.0) if d == 0 else values[i]
                fac[8 * d + 4 + i] = slopes[i] * normal

        def pair(k, carry):
            j = k // 2
            first = lax.rem(k, 2) * 2

            def add(s, accs):
                at = pl.ds(pl.multiple_of(s * 8, 8), 8)
                v0 = [fac[i, at, :] for i in range(4)]
                s0 = [fac[4 + i, at, :] for i in range(4)]
                v1 = fac[8 + j, at, :]
                s1 = fac[12 + j, at, :]
                out = []
                for e in range(2):
                    v2 = fac[16 + first + e, at, :]
                    s2 = fac[20 + first + e, at, :]
                    p = v1 * v2
                    q = s1 * v2 + v1 * s2
                    for i in range(4):
                        out.append(accs[len(out)] + (s0[i] * p + v0[i] * q))
                    for i in range(4):
                        out.append(accs[len(out)] + v0[i] * p)
                return tuple(out)

            zero = jnp.zeros((8, 128), F32)
            accs = lax.fori_loop(0, 16, add, (zero,) * 16, unroll=True)
            for e in range(2):
                for i in range(8):
                    row = 16 * i + 4 * j + first + e
                    nodes[pl.ds(row, 1), :] = jnp.sum(accs[8 * e + i], axis=0, keepdims=True)
            return carry

        lax.fori_loop(0, 8, pair, 0)
        tiles = nodes[...].T
        for c in range(per):
            target = g * per + c
            send[target, 0:cap, :] = tiles[c * cap:(c + 1) * cap]
            send[target, cap:cap + 8, :] = jnp.broadcast_to(idrows[target], (8, 128))

            @pl.when(target != me)
            def _():
                pltpu.make_async_remote_copy(
                    src_ref=send.at[target], dst_ref=recv.at[me],
                    send_sem=a2a_send, recv_sem=a2a_recv,
                    device_id=(target // n_grp, lax.rem(target, n_grp)), device_id_type=MESH,
                ).start()

            @pl.when(target == me)
            def _():
                recv[target] = send[target]
        return carry

    lax.fori_loop(0, groups, splat, 0)

    rowabs = jnp.zeros((64, 64), F32)
    for k in range(27):
        c = 0.5 * (coupling[k] + coupling[26 - k].T)
        rowabs = rowabs + jnp.abs(c)
        base = (2 - k // 9) * 192 + (2 - k // 3 % 3) * 64
        cs[base:base + 64, (k % 3) * 64:(k % 3) * 64 + 64] = c
    hi, lo = split(cs[...])
    chi[...] = hi
    clo[...] = lo
    rowabs = jnp.sum(rowabs, axis=1, keepdims=True) + 0.5
    mask = [occupied[c].astype(F32) for c in range(4)]

    everyone = pl.ds(0, devs - 1)
    pltpu.make_async_copy(recv.at[everyone], recv.at[everyone], a2a_recv).wait()
    pltpu.make_async_copy(send.at[everyone], send.at[everyone], a2a_send).wait()

    for k in range(groups):
        tiles = recv[k * per:(k + 1) * per, 0:cap, :].reshape(128, 128)
        hi, lo = split(tiles)
        weights[k * 128:(k + 1) * 128, 0:128] = hi
        weights[k * 128:(k + 1) * 128, 128:256] = lo
    ids = []
    for k in range(groups):
        row = recv[k * per, cap:cap + 1, :]
        for c in range(1, per):
            row = row + recv[k * per + c, cap:cap + 1, :]
        ids.append(row)
    ids = jnp.concatenate(ids, axis=1).astype(jnp.int32)
    for c in range(4):
        place = lax.broadcasted_iota(jnp.int32, (256, 1024), 0) + 256 * c
        hot = jnp.where(place == ids, 1.0, 0.0).astype(BF16)
        block = jnp.dot(hot, weights[...], preferred_element_type=F32)
        block = (block[:, 0:128] + block[:, 128:256]).T
        res[c] = block[0:64]
        diag[c] = rowabs + 4.0 * block[64:128]

    lane = lax.broadcasted_iota(jnp.int32, (64, 256), 1)

    def frame(fx, fy, m):
        up = jnp.where(lane == 0, 0.0, pltpu.roll(m, 1, 1))
        down = jnp.where(lane == 255, 0.0, pltpu.roll(m, 255, 1))
        hi, lo = split(jnp.concatenate([up, m, down], axis=0))
        xs = [x for x in range(2) if 0 <= fx - x <= 2]
        ys = [y for y in range(2) if 0 <= fy - y <= 2]
        size = 64 * len(ys)
        starts = [(2 - (fx - x)) * 192 + (2 - (fy - ys[0])) * 64 for x in xs]
        high = [chi[s:s + size, :] for s in starts]
        low = [clo[s:s + size, :] for s in starts]
        rows = size * len(xs)
        first = jnp.dot(jnp.concatenate(high + low, axis=0), hi, preferred_element_type=F32)
        second = jnp.dot(jnp.concatenate(high, axis=0), lo, preferred_element_type=F32)
        sums = first[0:rows] + (first[rows:2 * rows] + second)
        for a, x in enumerate(xs):
            for b, y in enumerate(ys):
                at = a * size + b * 64
                image[2 * x + y] += sums[at:at + 64]

    has = {
        ("x", 0): slab > 0, ("x", 3): slab < n_slab - 1,
        ("y", 0): grp > 0, ("y", 3): grp < n_grp - 1,
    }

    def both(a, b):
        return jnp.logical_and(a, b)

    def send_copy(t, src, f, dev):
        return pltpu.make_async_remote_copy(
            src_ref=src, dst_ref=halo_in.at[t, f], send_sem=halo_send.at[t, f],
            recv_sem=halo_recv.at[t, f], device_id=dev, device_id_type=MESH)

    def apply(t, src, dst):
        for c in range(4):
            halo_out[t, c] = mask[c] * src[c]
            image[c] = jnp.zeros((64, 256), F32)
        sends = []
        for y in (0, 1):
            sends.append((has["x", 3], halo_out.at[t, 2 + y], 0 * 4 + 1 + y, (slab + 1, grp)))
            sends.append((has["x", 0], halo_out.at[t, y], 3 * 4 + 1 + y, (slab - 1, grp)))
        for x in (0, 1):
            sends.append((has["y", 3], halo_out.at[t, 2 * x + 1], (1 + x) * 4, (slab, grp + 1)))
            sends.append((has["y", 0], halo_out.at[t, 2 * x], (1 + x) * 4 + 3, (slab, grp - 1)))
        for cond, ref, f, dev in sends:
            @pl.when(cond)
            def _():
                send_copy(t, ref, f, dev).start()
        for x in (0, 1):
            for y in (0, 1):
                frame(1 + x, 1 + y, halo_out[t, 2 * x + y])
        for fx in (0, 3):
            for y in (1, 0):
                f = fx * 4 + 1 + y
                corner = fx * 4 + (0 if y == 1 else 3)
                dev = (slab, grp + 1) if y == 1 else (slab, grp - 1)
                onward = has["y", 3] if y == 1 else has["y", 0]

                @pl.when(has["x", fx])
                def _():
                    send_copy(t, halo_in.at[t, f], f, (slab, grp)).wait_recv()

                @pl.when(both(has["x", fx], onward))
                def _():
                    send_copy(t, halo_in.at[t, f], corner, dev).start()
                sends.append((both(has["x", fx], onward), halo_in.at[t, f], corner, dev))
        for x in (0, 1):
            for fy in (0, 3):
                f = (1 + x) * 4 + fy

                @pl.when(has["y", fy])
                def _():
                    send_copy(t, halo_in.at[t, f], f, (slab, grp)).wait_recv()
                    frame(1 + x, fy, halo_in[t, f])
        for fx in (0, 3):
            for y in (0, 1):
                @pl.when(has["x", fx])
                def _():
                    frame(fx, 1 + y, halo_in[t, fx * 4 + 1 + y])
        for fx in (0, 3):
            for fy in (0, 3):
                f = fx * 4 + fy

                @pl.when(both(has["x", fx], has["y", fy]))
                def _():
                    send_copy(t, halo_in.at[t, f], f, (slab, grp)).wait_recv()
                    frame(fx, fy, halo_in[t, f])
        for c in range(4):
            dst[c] = diag[c] * src[c] - mask[c] * image[c]
        for cond, ref, f, dev in sends:
            @pl.when(cond)
            def _():
                send_copy(t, ref, f, dev).wait_send()

    def start_sum(t, pairs):
        for k, (a, b) in enumerate(pairs):
            acc = a[0] * b[0]
            for c in range(1, 4):
                acc = acc + a[c] * b[c]
            part[t, k:k + 1, :] = jnp.broadcast_to(total(acc), (1, 128))
        parts[t, me] = part[t]

        def go(k, carry):
            other = lax.rem(me + k, devs)
            pltpu.make_async_remote_copy(
                src_ref=part.at[t], dst_ref=parts.at[t, me], send_sem=sum_send.at[t],
                recv_sem=sum_recv.at[t],
                device_id=(other // n_grp, lax.rem(other, n_grp)), device_id_type=MESH,
            ).start()
            return carry

        lax.fori_loop(1, devs, go, 0)

    def end_sum(t):
        ref = parts.at[t, everyone]
        pltpu.make_async_copy(ref, ref, sum_recv.at[t]).wait()
        pltpu.make_async_copy(ref, ref, sum_send.at[t]).wait()
        whole = jnp.sum(parts[t], axis=0)
        return whole[0:1, 0:1], whole[1:2, 0:1], whole[2:3, 0:1]

    apply(0, res, wvec)
    start_sum(0, [(res, res), (res, wvec)])
    apply(1, wvec, zvec)
    rr, dq, _ = end_sum(0)
    alpha = rr / dq
    for c in range(4):
        d = res[c]
        q = wvec[c]
        z = zvec[c]
        dvec[c] = d
        qvec[c] = q
        zq[c] = z
        x_out[c] = alpha * d
        res[c] = d - alpha * q
        wvec[c] = q - alpha * z
    start_sum(1, [(res, res), (res, wvec), (res, qvec)])
    apply(2, wvec, zvec)
    new, delta, eps = end_sum(1)
    beta = new / rr
    dq = delta + 2.0 * beta * eps + beta * beta * dq
    rr = new
    alpha = rr / dq
    for c in range(4):
        r = res[c]
        w = wvec[c]
        d = r + beta * dvec[c]
        q = w + beta * qvec[c]
        z = zvec[c] + beta * zq[c]
        dvec[c] = d
        qvec[c] = q
        x_out[c] = x_out[c] + alpha * d
        res[c] = r - alpha * q
        wvec[c] = w - alpha * z
    start_sum(2, [(res, res), (res, wvec), (res, qvec)])
    new, delta, eps = end_sum(2)
    beta = new / rr
    dq = delta + 2.0 * beta * eps + beta * beta * dq
    alpha = new / dq
    for c in range(4):
        r = res[c]
        d = r + beta * dvec[c]
        q = wvec[c] + beta * qvec[c]
        x_out[c] = x_out[c] + alpha * d
        r_out[c] = r - alpha * q


def on_device(samples, block_ids, tile_counts, occupied, coupling):
    n_slab, n_grp = lax.axis_size("slab"), lax.axis_size("grp")
    devs = n_slab * n_grp
    size_x, size_y, size_z = occupied.shape
    slots = samples.shape[0]
    cap = slots // devs
    per = 128 // cap
    span_y = size_y * n_grp
    block_x = block_ids // (span_y * size_z)
    block_y = block_ids // size_z % span_y
    local = (block_x % size_x * size_y + block_y % size_y) * size_z + block_ids % size_z
    me = lax.axis_index("slab") * n_grp + lax.axis_index("grp")
    lanes = jnp.arange(128, dtype=jnp.int32) // cap
    idrows = jnp.tile(local.astype(F32).reshape(devs, cap), (1, per))
    idrows = jnp.where(lanes[None] == me % per, idrows, 0.0).reshape(devs, 1, 128)
    columns = size_x * size_y
    vec = pltpu.VMEM((columns, 64, size_z), F32)
    vmem = pl.BlockSpec(memory_space=pltpu.VMEM)
    shape = jax.ShapeDtypeStruct((columns, 64, size_z), F32)
    x, r = pl.pallas_call(
        functools.partial(kernel, n_slab, n_grp),
        out_shape=(shape, shape),
        in_specs=[vmem] * 5,
        out_specs=(vmem, vmem),
        scratch_shapes=[
            pltpu.VMEM((24, 128, 128), F32),
            pltpu.VMEM((128, 128), F32),
            pltpu.VMEM((devs, cap + 8, 128), F32),
            pltpu.VMEM((devs, cap + 8, 128), F32),
            pltpu.VMEM((576, 192), F32),
            pltpu.VMEM((576, 192), BF16),
            pltpu.VMEM((576, 192), BF16),
            vec,
            pltpu.VMEM((ITERS, 4, 64, size_z), F32),
            pltpu.VMEM((ITERS, 16, 64, size_z), F32),
            vec, vec, vec, vec, vec, vec, vec,
            pltpu.VMEM((ITERS, 8, 128), F32),
            pltpu.VMEM((ITERS, devs, 8, 128), F32),
            pltpu.VMEM((slots, 256), BF16),
            pltpu.SemaphoreType.DMA,
            pltpu.SemaphoreType.DMA,
            pltpu.SemaphoreType.DMA((ITERS, 16)),
            pltpu.SemaphoreType.DMA((ITERS, 16)),
            pltpu.SemaphoreType.DMA((ITERS,)),
            pltpu.SemaphoreType.DMA((ITERS,)),
        ],
        compiler_params=pltpu.CompilerParams(
            collective_id=0, has_side_effects=True, vmem_limit_bytes=40 * 1024 * 1024,
        ),
    )(samples, tile_counts.reshape(slots // 128, 1, 128), idrows,
      occupied.reshape(columns, 1, size_z), coupling)

    def shaped(v):
        return v.transpose(1, 0, 2).reshape(64, size_x, size_y, size_z)

    return shaped(x), shaped(r)


def solution(mesh):
    placed = (
        P(("slab", "grp"), None, None),
        P(("slab", "grp")),
        P(("slab", "grp")),
        P("slab", "grp", None),
        P(),
    )
    return jax.shard_map(
        on_device,
        mesh=mesh,
        in_specs=placed,
        out_specs=(P(None, "slab", "grp", None), P(None, "slab", "grp", None)),
        check_vma=False,
    )
```

profile of v0, /device:TPU:0, one launch (start us, length us, event | category | flops | bytes accessed | tf_op | source)
XLA Modules:
  0.0 73.5 jit_solution(2239637074547753188)
XLA Ops:
  0.6 0.0 copy-start
  0.6 0.0 copy-start.1
  0.7 0.8 %fusion.6 = f32[1024]{0:T(1024)S(1)} fusion(s32[1024]{0:T(1024)} %param.6), kind=kLoop, calls=%fused_computation.24 | loop fusion | flops 68608 | bytes 8192 | tf_op jit(solution)/shard_map/convert_element_type | solution.py:342
  1.5 0.7 reshape.67.occupied
  2.2 0.1 tile.10
  2.3 0.1 tile.12
  2.4 3.8 %copy.7.samples = f32[1024,6,128]{2,1,0:T(8,128)S(1)} copy(f32[1024,6,128]{2,0,1:T(8,128)} %param.5) | data formatting | bytes 6291456 | tf_op args[0]
  6.2 0.0 copy-done
  6.2 0.0 copy-done.1
  6.2 65.5 %shard_map.68 = (f32[4,64,256]{2,1,0:T(8,128)S(1)}, f32[4,64,256]{2,1,0:T(8,128)S(1)}) custom-call(f32[1024,6,128]{2,1,0:T(8,128)S(1)} %copy.7.samples, s32[8,1,128]{2,1,0:T(1,128)S(1)} %bitcast.9, f32[32,1,128]{2,1,0:T(1,128)S(1)} %broadcast_select_fusion.idrows, s32[4,1,256]{2,1,0:T(1,128)S(1)} %reshape.67.occupied, f32[27,64,64]{2,1,0:T(8,128)S(1)} %copy-done), custom_call_target="tpu_custom_call" | custom-call | tf_op jit(solution)/shard_map/pallas_call | solution.py:348
  71.7 0.9 %copy.8 = f32[64,2,2,256]{3,2,1,0:T(2,128)} copy(f32[64,2,2,256]{3,0,2,1:T(8,128)S(1)} %bitcast.8) | data formatting | bytes 524288
  72.6 0.9 %copy.9 = f32[64,2,2,256]{3,2,1,0:T(2,128)} copy(f32[64,2,2,256]{3,0,2,1:T(8,128)S(1)} %bitcast.7) | data formatting | bytes 524288
  (3 shorter events, 0.0 us)
Async XLA Ops:
  0.6 5.6 %copy-start = (f32[27,64,64]{2,1,0:T(8,128)S(1)}, f32[27,64,64]{2,1,0:T(8,128)}, u32[]{:S(2)}) copy-start(f32[27,64,64]{2,1,0:T(8,128)} %coupling.1) | copy-start | bytes 1327108
  0.6 5.6 %copy-start.1 = (s32[1024]{0:T(1024)S(1)}, s32[1024]{0:T(1024)}, u32[]{:S(2)}) copy-start(s32[1024]{0:T(1024)} %param.7) | copy-start | bytes 12292
where the time goes:
time: 73.7 us; the launch traced here: 73.5 us
  Pallas kernels  65.5 us (89%)
  local copies, waits for them, and re-layouts  6.5 us (9%)
  other arithmetic  0.81 us (1%)
    pallas_call x1, Pallas kernels, on_device(): pl.pallas_call(functools.partial(kernel, n_slab, n_grp), out_shape=(shape...  65.5 us
    unnamed x7, local copies, waits for them, and re-layouts  5.6 us

commit v1 on v0

--- a/solution.py
+++ b/solution.py
@@ -34,18 +34,30 @@
     return jnp.sum(jnp.sum(x, axis=0, keepdims=True), axis=1, keepdims=True)
 
 
-def kernel(n_slab, n_grp, samples, counts, idrows, occupied, coupling, x_out, r_out,
-           fac, nodes, send, recv, cs, chi, clo, diag, halo_out, halo_in, image, res, wvec,
-           zvec, dvec, qvec, zq, part, parts, weights, a2a_send, a2a_recv, halo_send, halo_recv,
+def kernel(n_slab, n_grp, samples, counts, block_ids, occupied, coupling, x_out, r_out,
+           held, fac, nodes, send, recv, cs, chi, clo, diag, halo_out, halo_in, image, res, wvec,
+           zvec, dvec, qvec, zq, part, parts, weights, held_sem, a2a_send, a2a_recv, halo_send, halo_recv,
            sum_send, sum_recv):
     devs = n_slab * n_grp
     cap = send.shape[1] - 8
     per = 128 // cap
-    groups = samples.shape[0] // 128
+    groups = samples.shape[1] // 128
+    size_x, size_y, size_z = occupied.shape
+    bits_z = size_z.bit_length() - 1
+    bits_y = (size_y * n_grp).bit_length() - 1
     slab = lax.axis_index("slab")
     grp = lax.axis_index("grp")
     me = slab * n_grp + grp
 
+    def group_of(step):
+        return lax.rem(me // per + groups // 2 + step, groups)
+
+    def fetch(g):
+        rows = pl.ds(pl.multiple_of(g * 128, 128), 128)
+        return pltpu.make_async_copy(samples.at[:, rows, :], held.at[g], held_sem.at[g])
+
+    for step in range(groups):
+        fetch(group_of(step)).start()
     part[...] = jnp.zeros_like(part)
     barrier = pltpu.get_barrier_semaphore()
 
@@ -59,12 +71,17 @@
     pl.semaphore_wait(barrier, devs - 1)
 
     def splat(step, carry):
-        g = lax.rem(me // per + groups // 2 + step, groups)
-        rows = pl.ds(pl.multiple_of(g * 128, 128), 128)
+        g = group_of(step)
+        fetch(g).wait()
+        name = block_ids[g]
+        z = jnp.bitwise_and(name, size_z - 1)
+        y = jnp.bitwise_and(jnp.right_shift(name, bits_z), size_y - 1)
+        x = jnp.bitwise_and(jnp.right_shift(name, bits_z + bits_y), size_x - 1)
+        name = jnp.broadcast_to(((x * size_y + y) * size_z + z).astype(F32), (8, 128))
         live = lax.broadcasted_iota(jnp.int32, (128, 128), 0) < counts[g]
         for d in range(3):
-            values, slopes = hats(4.0 * samples[rows, d, :].T)
-            normal = 4.0 * samples[rows, 3 + d, :].T
+            values, slopes = hats(4.0 * held[g, d].T)
+            normal = 4.0 * held[g, 3 + d].T
             if d == 0:
                 normal = jnp.where(live, normal, 0.0)
             for i in range(4):
@@ -106,7 +123,7 @@
         for c in range(per):
             target = g * per + c
             send[target, 0:cap, :] = tiles[c * cap:(c + 1) * cap]
-            send[target, cap:cap + 8, :] = jnp.broadcast_to(idrows[target], (8, 128))
+            send[target, cap:cap + 8, :] = name
 
             @pl.when(target != me)
             def _():
@@ -133,7 +150,20 @@
     chi[...] = hi
     clo[...] = lo
     rowabs = jnp.sum(rowabs, axis=1, keepdims=True) + 0.5
-    mask = [occupied[c].astype(F32) for c in range(4)]
+    mask = [occupied[c // 2, c % 2:c % 2 + 1, :].astype(F32) for c in range(4)]
+    has = {
+        ("x", 0): slab > 0, ("x", 3): slab < n_slab - 1,
+        ("y", 0): grp > 0, ("y", 3): grp < n_grp - 1,
+    }
+
+    for fx in range(4):
+        for fy in range(4):
+            sides = [has[k] for k in (("x", fx), ("y", fy)) if k in has]
+            if sides:
+                @pl.when(jnp.logical_not(functools.reduce(jnp.logical_and, sides)))
+                def _():
+                    for t in range(ITERS):
+                        halo_in[t, fx * 4 + fy] = jnp.zeros((64, 256), F32)
 
     everyone = pl.ds(0, devs - 1)
     pltpu.make_async_copy(recv.at[everyone], recv.at[everyone], a2a_recv).wait()
@@ -144,21 +174,17 @@
         hi, lo = split(tiles)
         weights[k * 128:(k + 1) * 128, 0:128] = hi
         weights[k * 128:(k + 1) * 128, 128:256] = lo
-    ids = []
-    for k in range(groups):
-        row = recv[k * per, cap:cap + 1, :]
-        for c in range(1, per):
-            row = row + recv[k * per + c, cap:cap + 1, :]
-        ids.append(row)
+    bits = cap.bit_length() - 1
+    lanes = jnp.right_shift(lax.broadcasted_iota(jnp.int32, (devs, 128), 1), bits)
+    source = jnp.bitwise_and(lax.broadcasted_iota(jnp.int32, (devs, 128), 0), per - 1)
+    names = jnp.where(lanes == lax.rem(me, per), recv[:, cap, :], 0.0)
+    shift = cap
+    while shift < 128:
+        names = names + pltpu.roll(names, shift, 1)
+        shift *= 2
+    names = jnp.where(lanes == source, names, 0.0)
+    ids = [jnp.sum(names[k * per:(k + 1) * per], axis=0, keepdims=True) for k in range(groups)]
     ids = jnp.concatenate(ids, axis=1).astype(jnp.int32)
-    for c in range(4):
-        place = lax.broadcasted_iota(jnp.int32, (256, 1024), 0) + 256 * c
-        hot = jnp.where(place == ids, 1.0, 0.0).astype(BF16)
-        block = jnp.dot(hot, weights[...], preferred_element_type=F32)
-        block = (block[:, 0:128] + block[:, 128:256]).T
-        res[c] = block[0:64]
-        diag[c] = rowabs + 4.0 * block[64:128]
-
     lane = lax.broadcasted_iota(jnp.int32, (64, 256), 1)
 
     def frame(fx, fy, m):
@@ -180,11 +206,6 @@
                 at = a * size + b * 64
                 image[2 * x + y] += sums[at:at + 64]
 
-    has = {
-        ("x", 0): slab > 0, ("x", 3): slab < n_slab - 1,
-        ("y", 0): grp > 0, ("y", 3): grp < n_grp - 1,
-    }
-
     def both(a, b):
         return jnp.logical_and(a, b)
 
@@ -193,66 +214,73 @@
             src_ref=src, dst_ref=halo_in.at[t, f], send_sem=halo_send.at[t, f],
             recv_sem=halo_recv.at[t, f], device_id=dev, device_id_type=MESH)
 
+    def column_sends(t, c):
+        x, y = c // 2, c % 2
+        ref = halo_out.at[t, c]
+        along_x = (slab + 1, grp) if x == 1 else (slab - 1, grp)
+        along_y = (slab, grp + 1) if y == 1 else (slab, grp - 1)
+        fx, fy = (0, 3)[x == 0], (0, 3)[y == 0]
+        return [(has["x", 3 - fx], ref, fx * 4 + 1 + y, along_x),
+                (has["y", 3 - fy], ref, (1 + x) * 4 + fy, along_y)]
+
+    def corner_send(t, fx, y):
+        f = fx * 4 + 1 + y
+        corner = fx * 4 + (0 if y == 1 else 3)
+        dev = (slab, grp + 1) if y == 1 else (slab, grp - 1)
+        cond = both(has["x", fx], has["y", 3 if y == 1 else 0])
+        return cond, halo_in.at[t, f], corner, dev
+
+    def start(t, cond, ref, f, dev):
+        @pl.when(cond)
+        def _():
+            send_copy(t, ref, f, dev).start()
+
+    def arrived(t, cond, f):
+        @pl.when(cond)
+        def _():
+            send_copy(t, halo_in.at[t, f], f, (slab, grp)).wait_recv()
+
+    def offer(t, c, value):
+        halo_out[t, c] = mask[c] * value
+        for send_one in column_sends(t, c):
+            start(t, *send_one)
+
     def apply(t, src, dst):
         for c in range(4):
-            halo_out[t, c] = mask[c] * src[c]
             image[c] = jnp.zeros((64, 256), F32)
-        sends = []
+        for c in range(4):
+            frame(1 + c // 2, 1 + c % 2, halo_out[t, c])
         for y in (0, 1):
-            sends.append((has["x", 3], halo_out.at[t, 2 + y], 0 * 4 + 1 + y, (slab + 1, grp)))
-            sends.append((has["x", 0], halo_out.at[t, y], 3 * 4 + 1 + y, (slab - 1, grp)))
-        for x in (0, 1):
-            sends.append((has["y", 3], halo_out.at[t, 2 * x + 1], (1 + x) * 4, (slab, grp + 1)))
-            sends.append((has["y", 0], halo_out.at[t, 2 * x], (1 + x) * 4 + 3, (slab, grp - 1)))
-        for cond, ref, f, dev in sends:
-            @pl.when(cond)
-            def _():
-                send_copy(t, ref, f, dev).start()
-        for x in (0, 1):
-            for y in (0, 1):
-                frame(1 + x, 1 + y, halo_out[t, 2 * x + y])
-        for fx in (0, 3):
-            for y in (1, 0):
-                f = fx * 4 + 1 + y
-                corner = fx * 4 + (0 if y == 1 else 3)
-                dev = (slab, grp + 1) if y == 1 else (slab, grp - 1)
-                onward = has["y", 3] if y == 1 else has["y", 0]
-
-                @pl.when(has["x", fx])
-                def _():
-                    send_copy(t, halo_in.at[t, f], f, (slab, grp)).wait_recv()
-
-                @pl.when(both(has["x", fx], onward))
-                def _():
-                    send_copy(t, halo_in.at[t, f], corner, dev).start()
-                sends.append((both(has["x", fx], onward), halo_in.at[t, f], corner, dev))
-        for x in (0, 1):
-            for fy in (0, 3):
-                f = (1 + x) * 4 + fy
-
-                @pl.when(has["y", fy])
-                def _():
-                    send_copy(t, halo_in.at[t, f], f, (slab, grp)).wait_recv()
-                    frame(1 + x, fy, halo_in[t, f])
+            for fx in (0, 3):
+                arrived(t, has["x", fx], fx * 4 + 1 + y)
+                start(t, *corner_send(t, fx, y))
+            for x in (0, 1):
+                arrived(t, has["y", 3 * y], (1 + x) * 4 + 3 * y)
+            for x in (0, 1):
+                frame(1 + x, 3 * y, halo_in[t, (1 + x) * 4 + 3 * y])
         for fx in (0, 3):
             for y in (0, 1):
-                @pl.when(has["x", fx])
-                def _():
-                    frame(fx, 1 + y, halo_in[t, fx * 4 + 1 + y])
+                frame(fx, 1 + y, halo_in[t, fx * 4 + 1 + y])
         for fx in (0, 3):
             for fy in (0, 3):
-                f = fx * 4 + fy
-
-                @pl.when(both(has["x", fx], has["y", fy]))
-                def _():
-                    send_copy(t, halo_in.at[t, f], f, (slab, grp)).wait_recv()
-                    frame(fx, fy, halo_in[t, f])
+                arrived(t, both(has["x", fx], has["y", fy]), fx * 4 + fy)
+        for fx in (0, 3):
+            for fy in (0, 3):
+                frame(fx, fy, halo_in[t, fx * 4 + fy])
         for c in range(4):
             dst[c] = diag[c] * src[c] - mask[c] * image[c]
-        for cond, ref, f, dev in sends:
-            @pl.when(cond)
-            def _():
-                send_copy(t, ref, f, dev).wait_send()
+        for c in range(4):
+            for cond, ref, f, dev in column_sends(t, c):
+                @pl.when(cond)
+                def _():
+                    send_copy(t, ref, f, dev).wait_send()
+        for fx in (0, 3):
+            for y in (0, 1):
+                cond, ref, f, dev = corner_send(t, fx, y)
+
+                @pl.when(cond)
+                def _():
+                    send_copy(t, ref, f, dev).wait_send()
 
     def start_sum(t, pairs):
         for k, (a, b) in enumerate(pairs):
@@ -280,7 +308,18 @@
         whole = jnp.sum(parts[t], axis=0)
         return whole[0:1, 0:1], whole[1:2, 0:1], whole[2:3, 0:1]
 
+    for c in range(4):
+        place = lax.broadcasted_iota(jnp.int32, (256, 1024), 0) + 256 * c
+        hot = jnp.where(place == ids, 1.0, 0.0).astype(BF16)
+        block = jnp.dot(hot, weights[...], preferred_element_type=F32)
+        block = (block[:, 0:128] + block[:, 128:256]).T
+        res[c] = block[0:64]
+        offer(0, c, block[0:64])
+        diag[c] = rowabs + 4.0 * block[64:128]
+
     apply(0, res, wvec)
+    for c in range(4):
+        offer(1, c, wvec[c])
     start_sum(0, [(res, res), (res, wvec)])
     apply(1, wvec, zvec)
     rr, dq, _ = end_sum(0)
@@ -294,7 +333,9 @@
         zq[c] = z
         x_out[c] = alpha * d
         res[c] = d - alpha * q
-        wvec[c] = q - alpha * z
+        w = q - alpha * z
+        wvec[c] = w
+        offer(2, c, w)
     start_sum(1, [(res, res), (res, wvec), (res, qvec)])
     apply(2, wvec, zvec)
     new, delta, eps = end_sum(1)
@@ -332,15 +373,6 @@
     size_x, size_y, size_z = occupied.shape
     slots = samples.shape[0]
     cap = slots // devs
-    per = 128 // cap
-    span_y = size_y * n_grp
-    block_x = block_ids // (span_y * size_z)
-    block_y = block_ids // size_z % span_y
-    local = (block_x % size_x * size_y + block_y % size_y) * size_z + block_ids % size_z
-    me = lax.axis_index("slab") * n_grp + lax.axis_index("grp")
-    lanes = jnp.arange(128, dtype=jnp.int32) // cap
-    idrows = jnp.tile(local.astype(F32).reshape(devs, cap), (1, per))
-    idrows = jnp.where(lanes[None] == me % per, idrows, 0.0).reshape(devs, 1, 128)
     columns = size_x * size_y
     vec = pltpu.VMEM((columns, 64, size_z), F32)
     vmem = pl.BlockSpec(memory_space=pltpu.VMEM)
@@ -348,9 +380,10 @@
     x, r = pl.pallas_call(
         functools.partial(kernel, n_slab, n_grp),
         out_shape=(shape, shape),
-        in_specs=[vmem] * 5,
+        in_specs=[pl.BlockSpec(memory_space=pl.ANY)] + [vmem] * 4,
         out_specs=(vmem, vmem),
         scratch_shapes=[
+            pltpu.VMEM((slots // 128, 6, 128, 128), F32),
             pltpu.VMEM((24, 128, 128), F32),
             pltpu.VMEM((128, 128), F32),
             pltpu.VMEM((devs, cap + 8, 128), F32),
@@ -365,6 +398,7 @@
             pltpu.VMEM((ITERS, 8, 128), F32),
             pltpu.VMEM((ITERS, devs, 8, 128), F32),
             pltpu.VMEM((slots, 256), BF16),
+            pltpu.SemaphoreType.DMA((slots // 128,)),
             pltpu.SemaphoreType.DMA,
             pltpu.SemaphoreType.DMA,
             pltpu.SemaphoreType.DMA((ITERS, 16)),
@@ -375,8 +409,8 @@
         compiler_params=pltpu.CompilerParams(
             collective_id=0, has_side_effects=True, vmem_limit_bytes=40 * 1024 * 1024,
         ),
-    )(samples, tile_counts.reshape(slots // 128, 1, 128), idrows,
-      occupied.reshape(columns, 1, size_z), coupling)
+    )(samples.transpose(1, 0, 2), tile_counts.reshape(slots // 128, 1, 128),
+      block_ids.reshape(slots // 128, 1, 128), occupied, coupling)
 
     def shaped(v):
         return v.transpose(1, 0, 2).reshape(64, size_x, size_y, size_z)

time: 73.7 us -> 69.3 us (0.940)
  Pallas kernels: 65.5 us -> 61.4 us
  other arithmetic: 0.81 us -> 0 us
    pallas_call x1, Pallas kernels: 65.5 us -> 61.4 us  [on_device(): pl.pallas_call(functools.partial(kernel, n_slab, n_grp), out_shape=(shape...]
    unnamed x7 -> x12, local copies, waits for them, and re-layouts: 5.6 us -> 6.92 us
    convert_element_type x1 -> x0, other arithmetic: 0.79 us -> none  [on_device(): idrows = jnp.tile(local.astype(F32).reshape(devs, cap), (1, per))]
where the time goes in v1:
time: 69.3 us; the launch traced here: 69 us
  Pallas kernels  61.4 us (89%)
  local copies, waits for them, and re-layouts  6.92 us (10%)
    pallas_call x1, Pallas kernels, on_device(): pl.pallas_call(functools.partial(kernel, n_slab, n_grp), out_shape=(shape...  61.4 us
    unnamed x12, local copies, waits for them, and re-layouts  6.92 us

profile of v1, /device:TPU:0, one launch (start us, length us, event | category | flops | bytes accessed | tf_op | source)
XLA Modules:
  0.0 69.0 jit_solution(17854637704393989664)
XLA Ops:
  0.6 0.0 copy-start
  0.6 1.9 %copy-done = f32[1024,6,128]{2,0,1:T(8,128)S(1)} copy-done((f32[1024,6,128]{2,0,1:T(8,128)S(1)}, f32[1024,6,128]{2,0,1:T(8,128)}, u32[]{:S(2)}) %copy-start) | copy-done | bytes 3145752
  2.5 0.0 copy-start.1
  2.5 1.2 %copy-done.1 = f32[27,64,64]{2,1,0:T(8,128)S(1)} copy-done((f32[27,64,64]{2,1,0:T(8,128)S(1)}, f32[27,64,64]{2,1,0:T(8,128)}, u32[]{:S(2)}) %copy-start.1) | copy-done | bytes 442392
  3.7 0.0 copy-start.2
  3.7 0.7 copy-done.2
  4.4 0.0 copy-start.3
  4.4 0.7 copy-done.3
  5.1 0.0 copy-start.4
  5.1 0.7 copy-done.4
  5.8 61.4 %shard_map.68 = (f32[4,64,256]{2,1,0:T(8,128)S(1)}, f32[4,64,256]{2,1,0:T(8,128)S(1)}) custom-call(f32[6,1024,128]{2,1,0:T(8,128)S(1)} %bitcast.9, s32[8,1,128]{2,1,0:T(1,128)S(1)} %bitcast.12, s32[8,1,128]{2,1,0:T(1,128)S(1)} %bitcast.13, s32[2,2,256]{2,1,0:T(2,128)S(1)} %copy-done.4, f32[27,64,64]{2,1,0:T(8,128)S(1)} %copy-done.1), custom_call_target="tpu_custom_call" | custom-call | tf_op jit(solution)/shard_map/pallas_call | solution.py:380
  67.2 0.9 %copy.7 = f32[64,2,2,256]{3,2,1,0:T(2,128)} copy(f32[64,2,2,256]{3,0,2,1:T(8,128)S(1)} %bitcast.11) | data formatting | bytes 524288
  68.1 0.9 %copy.8 = f32[64,2,2,256]{3,2,1,0:T(2,128)} copy(f32[64,2,2,256]{3,0,2,1:T(8,128)S(1)} %bitcast.10) | data formatting | bytes 524288
Async XLA Ops:
  0.6 1.9 %copy-start = (f32[1024,6,128]{2,0,1:T(8,128)S(1)}, f32[1024,6,128]{2,0,1:T(8,128)}, u32[]{:S(2)}) copy-start(f32[1024,6,128]{2,0,1:T(8,128)} %param.5) | copy-start | bytes 9437188
  2.5 1.2 %copy-start.1 = (f32[27,64,64]{2,1,0:T(8,128)S(1)}, f32[27,64,64]{2,1,0:T(8,128)}, u32[]{:S(2)}) copy-start(f32[27,64,64]{2,1,0:T(8,128)} %coupling.1) | copy-start | bytes 1327108
  3.7 0.7 copy-start.2
  4.4 0.7 copy-start.3
  5.1 0.7 copy-start.4

commit v2 on v1

--- a/solution.py
+++ b/solution.py
@@ -25,6 +25,19 @@
     return values, slopes
 
 
+def fold(rows):
+    place = lax.broadcasted_iota(jnp.int32, (8, 128), 0)
+    step = 1
+    while len(rows) > 1:
+        keep = jnp.bitwise_and(place, step) == 0
+        rows = [
+            jnp.where(keep, a, b) + pltpu.roll(jnp.where(keep, b, a), 8 - step, 0)
+            for a, b in zip(rows[0::2], rows[1::2])
+        ]
+        step *= 2
+    return rows[0]
+
+
 def split(x):
     hi = x.astype(BF16)
     return hi, (x - hi.astype(F32)).astype(BF16)
@@ -34,10 +47,11 @@
     return jnp.sum(jnp.sum(x, axis=0, keepdims=True), axis=1, keepdims=True)
 
 
-def kernel(n_slab, n_grp, samples, counts, block_ids, occupied, coupling, x_out, r_out,
-           held, fac, nodes, send, recv, cs, chi, clo, diag, halo_out, halo_in, image, res, wvec,
-           zvec, dvec, qvec, zq, part, parts, weights, held_sem, a2a_send, a2a_recv, halo_send, halo_recv,
-           sum_send, sum_recv):
+def kernel(n_slab, n_grp, samples, *refs):
+    (count_in, name_in, occupied_in, coupling_in, x_out, r_out, counts, block_ids, occupied,
+     coupling, held, fac, nodes, send, recv, cs, chi, clo, diag, halo_out, halo_in, image, res, wvec,
+     zvec, dvec, qvec, zq, part, parts, weights, held_sem, a2a_send, a2a_recv, halo_send, halo_recv,
+     sum_send, sum_recv, in_sem) = refs
     devs = n_slab * n_grp
     cap = send.shape[1] - 8
     per = 128 // cap
@@ -56,8 +70,15 @@
         rows = pl.ds(pl.multiple_of(g * 128, 128), 128)
         return pltpu.make_async_copy(samples.at[:, rows, :], held.at[g], held_sem.at[g])
 
+    small = [(count_in, counts), (name_in, block_ids), (occupied_in, occupied),
+             (coupling_in, coupling)]
+    small = [pltpu.make_async_copy(a, b, in_sem.at[k]) for k, (a, b) in enumerate(small)]
+    small[0].start()
+    small[1].start()
     for step in range(groups):
         fetch(group_of(step)).start()
+    small[2].start()
+    small[3].start()
     part[...] = jnp.zeros_like(part)
     barrier = pltpu.get_barrier_semaphore()
 
@@ -69,6 +90,9 @@
 
     lax.fori_loop(1, devs, greet, 0)
     pl.semaphore_wait(barrier, devs - 1)
+
+    small[0].wait()
+    small[1].wait()
 
     def splat(step, carry):
         g = group_of(step)
@@ -89,33 +113,31 @@
                 fac[8 * d + 4 + i] = slopes[i] * normal
 
         def pair(k, carry):
-            j = k // 2
+            i = k // 2
             first = lax.rem(k, 2) * 2
 
             def add(s, accs):
                 at = pl.ds(pl.multiple_of(s * 8, 8), 8)
-                v0 = [fac[i, at, :] for i in range(4)]
-                s0 = [fac[4 + i, at, :] for i in range(4)]
-                v1 = fac[8 + j, at, :]
-                s1 = fac[12 + j, at, :]
-                out = []
+                v0 = fac[i, at, :]
+                s0 = fac[4 + i, at, :]
+                v2 = [fac[16 + l, at, :] for l in range(4)]
+                s2 = [fac[20 + l, at, :] for l in range(4)]
+                rhs, dens = [], []
                 for e in range(2):
-                    v2 = fac[16 + first + e, at, :]
-                    s2 = fac[20 + first + e, at, :]
-                    p = v1 * v2
-                    q = s1 * v2 + v1 * s2
-                    for i in range(4):
-                        out.append(accs[len(out)] + (s0[i] * p + v0[i] * q))
-                    for i in range(4):
-                        out.append(accs[len(out)] + v0[i] * p)
-                return tuple(out)
+                    v1 = fac[8 + first + e, at, :]
+                    s1 = fac[12 + first + e, at, :]
+                    p = v0 * v1
+                    q = s0 * v1 + v0 * s1
+                    for l in range(4):
+                        rhs.append(accs[4 * e + l] + (v2[l] * q + s2[l] * p))
+                        dens.append(accs[8 + 4 * e + l] + v2[l] * p)
+                return tuple(rhs + dens)
 
             zero = jnp.zeros((8, 128), F32)
             accs = lax.fori_loop(0, 16, add, (zero,) * 16, unroll=True)
-            for e in range(2):
-                for i in range(8):
-                    row = 16 * i + 4 * j + first + e
-                    nodes[pl.ds(row, 1), :] = jnp.sum(accs[8 * e + i], axis=0, keepdims=True)
+            base = pl.multiple_of(8 * k, 8)
+            nodes[pl.ds(base, 8), :] = fold(accs[0:8])
+            nodes[pl.ds(64 + base, 8), :] = fold(accs[8:16])
             return carry
 
         lax.fori_loop(0, 8, pair, 0)
@@ -139,6 +161,9 @@
         return carry
 
     lax.fori_loop(0, groups, splat, 0)
+
+    small[2].wait()
+    small[3].wait()
 
     rowabs = jnp.zeros((64, 64), F32)
     for k in range(27):
@@ -380,9 +405,13 @@
     x, r = pl.pallas_call(
         functools.partial(kernel, n_slab, n_grp),
         out_shape=(shape, shape),
-        in_specs=[pl.BlockSpec(memory_space=pl.ANY)] + [vmem] * 4,
+        in_specs=[pl.BlockSpec(memory_space=pl.ANY)] * 5,
         out_specs=(vmem, vmem),
         scratch_shapes=[
+            pltpu.VMEM((slots // 128, 1, 128), jnp.int32),
+            pltpu.VMEM((slots // 128, 1, 128), jnp.int32),
+            pltpu.VMEM(occupied.shape, jnp.int32),
+            pltpu.VMEM(coupling.shape, F32),
             pltpu.VMEM((slots // 128, 6, 128, 128), F32),
             pltpu.VMEM((24, 128, 128), F32),
             pltpu.VMEM((128, 128), F32),
@@ -405,9 +434,10 @@
             pltpu.SemaphoreType.DMA((ITERS, 16)),
             pltpu.SemaphoreType.DMA((ITERS,)),
             pltpu.SemaphoreType.DMA((ITERS,)),
+            pltpu.SemaphoreType.DMA((4,)),
         ],
         compiler_params=pltpu.CompilerParams(
-            collective_id=0, has_side_effects=True, vmem_limit_bytes=40 * 1024 * 1024,
+            collective_id=0, has_side_effects=True, vmem_limit_bytes=60 * 1024 * 1024,
         ),
     )(samples.transpose(1, 0, 2), tile_counts.reshape(slots // 128, 1, 128),
       block_ids.reshape(slots // 128, 1, 128), occupied, coupling)

time: 69.3 us -> 67.7 us (0.977)
  local copies, waits for them, and re-layouts: 6.92 us -> 3.71 us
  Pallas kernels: 61.4 us -> 63.1 us
    unnamed x12 -> x2, local copies, waits for them, and re-layouts: 6.92 us -> 3.71 us
    pallas_call x1, Pallas kernels: 61.4 us -> 63.1 us  [on_device(): pl.pallas_call(functools.partial(kernel, n_slab, n_grp), out_shape=(shape...]
where the time goes in v2:
time: 67.7 us; the launch traced here: 67.5 us
  Pallas kernels  63.1 us (93%)
  local copies, waits for them, and re-layouts  3.71 us (5%)
    pallas_call x1, Pallas kernels, on_device(): pl.pallas_call(functools.partial(kernel, n_slab, n_grp), out_shape=(shape...  63.1 us
    unnamed x2, local copies, waits for them, and re-layouts  3.71 us

profile of v2, /device:TPU:0, one launch (start us, length us, event | category | flops | bytes accessed | tf_op | source)
XLA Modules:
  0.0 67.5 jit_solution(8658601787415900090)
XLA Ops:
  0.6 63.1 %shard_map.68 = (f32[4,64,256]{2,1,0:T(8,128)}, f32[4,64,256]{2,1,0:T(8,128)}) custom-call(f32[6,1024,128]{2,1,0:T(8,128)} %bitcast.9, s32[8,1,128]{2,1,0:T(1,128)} %bitcast.12, s32[8,1,128]{2,1,0:T(1,128)} %bitcast.13, s32[2,2,256]{2,1,0:T(2,128)} %refs_2_.1, f32[27,64,64]{2,1,0:T(8,128)} %refs_3_.1), custom_call_target="tpu_custom_call" | custom-call | tf_op jit(solution)/shard_map/pallas_call | solution.py:405
  63.8 1.9 %copy.7 = f32[64,2,2,256]{3,2,1,0:T(2,128)} copy(f32[64,2,2,256]{3,0,2,1:T(8,128)} %bitcast.11) | data formatting | bytes 524288
  65.6 1.9 %copy.8 = f32[64,2,2,256]{3,2,1,0:T(2,128)} copy(f32[64,2,2,256]{3,0,2,1:T(8,128)} %bitcast.10) | data formatting | bytes 524288

commit v3 on v2

--- a/solution.py
+++ b/solution.py
@@ -49,13 +49,14 @@
 
 def kernel(n_slab, n_grp, samples, *refs):
     (count_in, name_in, occupied_in, coupling_in, x_out, r_out, counts, block_ids, occupied,
-     coupling, held, fac, nodes, send, recv, cs, chi, clo, diag, halo_out, halo_in, image, res, wvec,
+     coupling, held, fac, nodes, send, recv, cs, deep, diag, halo_out, halo_in, image, res, wvec,
      zvec, dvec, qvec, zq, part, parts, weights, held_sem, a2a_send, a2a_recv, halo_send, halo_recv,
      sum_send, sum_recv, in_sem) = refs
     devs = n_slab * n_grp
-    cap = send.shape[1] - 8
+    cap = send.shape[1] - 1
     per = 128 // cap
     groups = samples.shape[1] // 128
+    share = groups // n_slab
     size_x, size_y, size_z = occupied.shape
     bits_z = size_z.bit_length() - 1
     bits_y = (size_y * n_grp).bit_length() - 1
@@ -64,7 +65,9 @@
     me = slab * n_grp + grp
 
     def group_of(step):
-        return lax.rem(me // per + groups // 2 + step, groups)
+        k = step // share
+        away = jnp.where(k < n_slab // 2, k + n_slab // 2, n_slab - 1 - k)
+        return lax.rem(slab + away, n_slab) * share + lax.rem(step, share)
 
     def fetch(g):
         rows = pl.ds(pl.multiple_of(g * 128, 128), 128)
@@ -89,7 +92,6 @@
         return carry
 
     lax.fori_loop(1, devs, greet, 0)
-    pl.semaphore_wait(barrier, devs - 1)
 
     small[0].wait()
     small[1].wait()
@@ -101,7 +103,7 @@
         z = jnp.bitwise_and(name, size_z - 1)
         y = jnp.bitwise_and(jnp.right_shift(name, bits_z), size_y - 1)
         x = jnp.bitwise_and(jnp.right_shift(name, bits_z + bits_y), size_x - 1)
-        name = jnp.broadcast_to(((x * size_y + y) * size_z + z).astype(F32), (8, 128))
+        name = ((x * size_y + y) * size_z + z).astype(F32)
         live = lax.broadcasted_iota(jnp.int32, (128, 128), 0) < counts[g]
         for d in range(3):
             values, slopes = hats(4.0 * held[g, d].T)
@@ -142,10 +144,15 @@
 
         lax.fori_loop(0, 8, pair, 0)
         tiles = nodes[...].T
+
+        @pl.when(step == 0)
+        def _():
+            pl.semaphore_wait(barrier, devs - 1)
+
         for c in range(per):
             target = g * per + c
             send[target, 0:cap, :] = tiles[c * cap:(c + 1) * cap]
-            send[target, cap:cap + 8, :] = name
+            send[target, cap:cap + 1, :] = name
 
             @pl.when(target != me)
             def _():
@@ -172,8 +179,9 @@
         base = (2 - k // 9) * 192 + (2 - k // 3 % 3) * 64
         cs[base:base + 64, (k % 3) * 64:(k % 3) * 64 + 64] = c
     hi, lo = split(cs[...])
-    chi[...] = hi
-    clo[...] = lo
+    deep[:, 0:192] = hi
+    deep[:, 192:384] = hi
+    deep[:, 384:576] = lo
     rowabs = jnp.sum(rowabs, axis=1, keepdims=True) + 0.5
     mask = [occupied[c // 2, c % 2:c % 2 + 1, :].astype(F32) for c in range(4)]
     has = {
@@ -220,12 +228,8 @@
         ys = [y for y in range(2) if 0 <= fy - y <= 2]
         size = 64 * len(ys)
         starts = [(2 - (fx - x)) * 192 + (2 - (fy - ys[0])) * 64 for x in xs]
-        high = [chi[s:s + size, :] for s in starts]
-        low = [clo[s:s + size, :] for s in starts]
-        rows = size * len(xs)
-        first = jnp.dot(jnp.concatenate(high + low, axis=0), hi, preferred_element_type=F32)
-        second = jnp.dot(jnp.concatenate(high, axis=0), lo, preferred_element_type=F32)
-        sums = first[0:rows] + (first[rows:2 * rows] + second)
+        left = jnp.concatenate([deep[s:s + size, :] for s in starts], axis=0)
+        sums = jnp.dot(left, jnp.concatenate([hi, lo, hi], axis=0), preferred_element_type=F32)
         for a, x in enumerate(xs):
             for b, y in enumerate(ys):
                 at = a * size + b * 64
@@ -415,11 +419,10 @@
             pltpu.VMEM((slots // 128, 6, 128, 128), F32),
             pltpu.VMEM((24, 128, 128), F32),
             pltpu.VMEM((128, 128), F32),
-            pltpu.VMEM((devs, cap + 8, 128), F32),
-            pltpu.VMEM((devs, cap + 8, 128), F32),
+            pltpu.VMEM((devs, cap + 1, 128), F32),
+            pltpu.VMEM((devs, cap + 1, 128), F32),
             pltpu.VMEM((576, 192), F32),
-            pltpu.VMEM((576, 192), BF16),
-            pltpu.VMEM((576, 192), BF16),
+            pltpu.VMEM((576, 576), BF16),
             vec,
             pltpu.VMEM((ITERS, 4, 64, size_z), F32),
             pltpu.VMEM((ITERS, 16, 64, size_z), F32),

time: 67.7 us -> 63.9 us (0.944)
  Pallas kernels: 63.1 us -> 59.4 us
    pallas_call x1, Pallas kernels: 63.1 us -> 59.4 us  [on_device(): pl.pallas_call(functools.partial(kernel, n_slab, n_grp), out_shape=(shape...]
where the time goes in v3:
time: 63.9 us; the launch traced here: 63.8 us
  Pallas kernels  59.4 us (93%)
  local copies, waits for them, and re-layouts  3.71 us (6%)
  between operations  0.64 us (1%)
    pallas_call x1, Pallas kernels, on_device(): pl.pallas_call(functools.partial(kernel, n_slab, n_grp), out_shape=(shape...  59.4 us
    unnamed x2, local copies, waits for them, and re-layouts  3.71 us

profile of v3, /device:TPU:0, one launch (start us, length us, event | category | flops | bytes accessed | tf_op | source)
XLA Modules:
  0.0 63.8 jit_solution(210228003877595916)
XLA Ops:
  0.6 59.4 %shard_map.68 = (f32[4,64,256]{2,1,0:T(8,128)}, f32[4,64,256]{2,1,0:T(8,128)}) custom-call(f32[6,1024,128]{2,1,0:T(8,128)} %bitcast.9, s32[8,1,128]{2,1,0:T(1,128)} %bitcast.12, s32[8,1,128]{2,1,0:T(1,128)} %bitcast.13, s32[2,2,256]{2,1,0:T(2,128)} %refs_2_.1, f32[27,64,64]{2,1,0:T(8,128)} %refs_3_.1), custom_call_target="tpu_custom_call" | custom-call | tf_op jit(solution)/shard_map/pallas_call | solution.py:409
  60.1 1.9 %copy.7 = f32[64,2,2,256]{3,2,1,0:T(2,128)} copy(f32[64,2,2,256]{3,0,2,1:T(8,128)} %bitcast.11) | data formatting | bytes 524288
  61.9 1.9 %copy.8 = f32[64,2,2,256]{3,2,1,0:T(2,128)} copy(f32[64,2,2,256]{3,0,2,1:T(8,128)} %bitcast.10) | data formatting | bytes 524288

commit v4 on v3

--- a/solution.py
+++ b/solution.py
@@ -82,7 +82,6 @@
         fetch(group_of(step)).start()
     small[2].start()
     small[3].start()
-    part[...] = jnp.zeros_like(part)
     barrier = pltpu.get_barrier_semaphore()
 
     def greet(k, carry):
@@ -142,7 +141,7 @@
             nodes[pl.ds(64 + base, 8), :] = fold(accs[8:16])
             return carry
 
-        lax.fori_loop(0, 8, pair, 0)
+        lax.fori_loop(0, 8, pair, 0, unroll=True)
         tiles = nodes[...].T
 
         @pl.when(step == 0)
@@ -312,12 +311,15 @@
                     send_copy(t, ref, f, dev).wait_send()
 
     def start_sum(t, pairs):
+        row = jnp.zeros((1, 128), F32)
+        column = lax.broadcasted_iota(jnp.int32, (1, 128), 1)
         for k, (a, b) in enumerate(pairs):
             acc = a[0] * b[0]
             for c in range(1, 4):
                 acc = acc + a[c] * b[c]
-            part[t, k:k + 1, :] = jnp.broadcast_to(total(acc), (1, 128))
-        parts[t, me] = part[t]
+            row = jnp.where(column == k, total(acc), row)
+        part[t] = row
+        parts[t, me] = row
 
         def go(k, carry):
             other = lax.rem(me + k, devs)
@@ -335,7 +337,7 @@
         pltpu.make_async_copy(ref, ref, sum_recv.at[t]).wait()
         pltpu.make_async_copy(ref, ref, sum_send.at[t]).wait()
         whole = jnp.sum(parts[t], axis=0)
-        return whole[0:1, 0:1], whole[1:2, 0:1], whole[2:3, 0:1]
+        return whole[:, 0:1], whole[:, 1:2], whole[:, 2:3]
 
     for c in range(4):
         place = lax.broadcasted_iota(jnp.int32, (256, 1024), 0) + 256 * c
@@ -427,8 +429,8 @@
             pltpu.VMEM((ITERS, 4, 64, size_z), F32),
             pltpu.VMEM((ITERS, 16, 64, size_z), F32),
             vec, vec, vec, vec, vec, vec, vec,
-            pltpu.VMEM((ITERS, 8, 128), F32),
-            pltpu.VMEM((ITERS, devs, 8, 128), F32),
+            pltpu.VMEM((ITERS, 1, 128), F32),
+            pltpu.VMEM((ITERS, devs, 1, 128), F32),
             pltpu.VMEM((slots, 256), BF16),
             pltpu.SemaphoreType.DMA((slots // 128,)),
             pltpu.SemaphoreType.DMA,

time: 63.9 us -> 59.7 us (0.934)
  Pallas kernels: 59.4 us -> 55.1 us
    pallas_call x1, Pallas kernels: 59.4 us -> 55.1 us  [on_device(): pl.pallas_call(functools.partial(kernel, n_slab, n_grp), out_shape=(shape...]
where the time goes in v4:
time: 59.7 us; the launch traced here: 59.5 us
  Pallas kernels  55.1 us (92%)
  local copies, waits for them, and re-layouts  3.71 us (6%)
  between operations  0.64 us (1%)
    pallas_call x1, Pallas kernels, on_device(): pl.pallas_call(functools.partial(kernel, n_slab, n_grp), out_shape=(shape...  55.1 us
    unnamed x2, local copies, waits for them, and re-layouts  3.71 us

profile of v4, /device:TPU:0, one launch (start us, length us, event | category | flops | bytes accessed | tf_op | source)
XLA Modules:
  0.0 59.5 jit_solution(17863023182465411644)
XLA Ops:
  0.6 55.1 %shard_map.68 = (f32[4,64,256]{2,1,0:T(8,128)}, f32[4,64,256]{2,1,0:T(8,128)}) custom-call(f32[6,1024,128]{2,1,0:T(8,128)} %bitcast.9, s32[8,1,128]{2,1,0:T(1,128)} %bitcast.12, s32[8,1,128]{2,1,0:T(1,128)} %bitcast.13, s32[2,2,256]{2,1,0:T(2,128)} %refs_2_.1, f32[27,64,64]{2,1,0:T(8,128)} %refs_3_.1), custom_call_target="tpu_custom_call" | custom-call | tf_op jit(solution)/shard_map/pallas_call | solution.py:411
  55.8 1.9 %copy.7 = f32[64,2,2,256]{3,2,1,0:T(2,128)} copy(f32[64,2,2,256]{3,0,2,1:T(8,128)} %bitcast.11) | data formatting | bytes 524288
  57.6 1.9 %copy.8 = f32[64,2,2,256]{3,2,1,0:T(2,128)} copy(f32[64,2,2,256]{3,0,2,1:T(8,128)} %bitcast.10) | data formatting | bytes 524288
